TPU v7x, 32 devices: a whole 2x2x4 slice. The times are simulated.
32 devices in a mesh: dp: 16 (over z, y, x), fsdp: 2 (over core).
Axes of the slice: x: 2, y: 2, z: 4, core: 2. Of those that a mesh axis runs over, the one named last changes fastest.
Arguments:
- inputs: bfloat16 [12288, 8192], P('dp', 'fsdp'), may hold values from -6 to 6
- grad_out: bfloat16 [12288, 14336], P('dp', 'fsdp'), may hold values from -0.053955078 to 0.053955078
- projector: bfloat16 [8192, 256], P('fsdp', 'dp'), may hold values from -0.0625 to 0.0625
- moment: float32 [14336, 256], P(('fsdp', 'dp')), may hold values from -3 to 3
- second: float32 [14336, 256], P(('fsdp', 'dp')), may hold values from 0.05 to 2
Outputs:
- update: bfloat16 [2, 7168, 8192], P(None, 'dp', 'fsdp')
- moment_new: float32 [14336, 256], P(('fsdp', 'dp'))
- second_new: float32 [14336, 256], P(('fsdp', 'dp'))
All inputs are finite; a program needn't handle non-finite values.
Results may differ from a plain program's by a relative error of at most 0.005.
Values may be sent and summed in bfloat16 or wider, within the bound.
No kernel may reach another device: no remote copies, remote signals or barrier semaphores. Data moves between devices by JAX's collectives and lax.ppermute only.
A program may use at most 64 MiB of HBM per device.

v0:
```python
import jax
import jax.numpy as jnp
from jax import lax
from jax.sharding import PartitionSpec as P

STEP = 10


BETA_FIRST = 0.9
BETA_SECOND = 0.999
EPSILON = 1e-08


def adam_direction(grad_sub, moment, second):
    moment_new = BETA_FIRST * moment + (1.0 - BETA_FIRST) * grad_sub
    second_new = BETA_SECOND * second + (1.0 - BETA_SECOND) * grad_sub * grad_sub
    first_hat = moment_new / (1.0 - BETA_FIRST**STEP)
    second_hat = second_new / (1.0 - BETA_SECOND**STEP)
    direction = (first_hat / (jnp.sqrt(second_hat) + EPSILON)).astype(jnp.bfloat16)
    return (moment_new, second_new, direction)


def local(inputs, grad_out, projector, moment, second):
    full_basis = lax.all_gather(projector, "dp", axis=1, tiled=True)
    local_proj = jnp.dot(inputs, full_basis, preferred_element_type=jnp.float32)
    projected = lax.psum(local_proj, "fsdp").astype(jnp.bfloat16)
    owned_units = grad_out.shape[1] // lax.axis_size("dp")
    block_terms = lax.dot_general(
        grad_out, projected, (((0,), (0,)), ((), ())), preferred_element_type=jnp.float32
    )
    block_total = lax.psum(block_terms, "dp")
    owned_start = lax.axis_index("dp") * owned_units
    grad_sub = lax.dynamic_slice_in_dim(block_total, owned_start, owned_units, 0)
    moment_new, second_new, direction = adam_direction(grad_sub, moment, second)
    gathered = lax.all_gather(direction, "fsdp", axis=0, tiled=True)
    decoded = lax.dot_general(
        gathered, full_basis, (((1,), (1,)), ((), ())), preferred_element_type=jnp.float32
    )
    blocks = lax.axis_size("fsdp")
    update = decoded.astype(jnp.bfloat16).reshape(blocks, owned_units, decoded.shape[1])
    return (update, moment_new, second_new)


def solution(mesh):
    return jax.shard_map(
        local,
        mesh=mesh,
        in_specs=(
            P("dp", "fsdp"),
            P("dp", "fsdp"),
            P("fsdp", "dp"),
            P(("fsdp", "dp"), None),
            P(("fsdp", "dp"), None),
        ),
        out_specs=(P(None, "dp", "fsdp"), P(("fsdp", "dp"), None), P(("fsdp", "dp"), None)),
        check_vma=False,
    )
```

profile of v0, /device:TPU:0, one launch (start us, length us, event | category | flops | bytes accessed | tf_op | source)
XLA Modules:
  0.0 346.2 jit_solution(14611101976486536036)
XLA Ops:
  7.2 0.0 all-gather.2.cloned.1.call-start
  7.2 0.7 all-gather.2.cloned.1.call-update
  7.9 0.0 all-reduce.3.cloned.1.call-start
  7.9 66.3 %all-gather.2.cloned.1.call-done = bf16[4096,256]{0,1:T(8,128)(2,1)} async-done(((bf16[4096,16]{0,1:T(8,128)(2,1)}), bf16[4096,256]{0,1:T(8,128)(2,1)}) %all-gather.2.cloned.1.call-update) | async-done | bytes 2097168 | tf_op jit(solution)/shard_map/all_gather | solution.py:24
  74.2 5.2 %fusion.3 = f32[768,256]{1,0:T(8,128)S(1)} fusion(bf16[768,4096]{1,0:T(8,128)(2,1)} %param.5, bf16[4096,256]{0,1:T(8,128)(2,1)} %all-gather.2.cloned.1.call-done), kind=kOutput, calls=%fused_computation.7 | convolution fusion | flops 1610612736 | bytes 9175040 | tf_op jit(solution)/shard_map/dot_general | solution.py:25
  79.5 5.5 %all-reduce.4 = bf16[768,256]{1,0:T(8,128)(2,1)S(1)} all-reduce(f32[768,256]{1,0:T(8,128)S(1)} %fusion.3), channel_id=1, replica_groups=mesh['dp'=16,'fsdp'=2] {'fsdp'}, use_global_device_ids=true, to_apply=%region_0.0 | all-reduce | flops 196608 | bytes 1179648 | tf_op jit(solution)/shard_map/psum | solution.py:26
  85.0 9.4 %convolution_bitcast_fusion = f32[7168,256]{0,1:T(8,128)} fusion(bf16[768,7168]{1,0:T(8,128)(2,1)} %param.6, bf16[768,256]{1,0:T(8,128)(2,1)S(1)} %all-reduce.4), kind=kOutput, calls=%fused_computation | convolution fusion | flops 2818572288 | bytes 18743296 | tf_op jit(solution)/shard_map/dot_general | solution.py:28
  94.3 0.0 copy-start.1
  94.3 0.0 copy-start
  94.3 0.0 all-reduce.3.cloned.1.call-update
  94.4 1.0 copy-done.1
  95.3 0.2 copy.12
  95.5 1.2 copy.13
  96.8 228.7 %all-reduce.3.cloned.1.call-done = f32[7168,256]{0,1:T(8,128)} async-done(((f32[7168,256]{0,1:T(8,128)}), f32[7168,256]{0,1:T(8,128)}) %all-reduce.3.cloned.1.call-update) | async-done | bytes 7340048 | tf_op jit(solution)/shard_map/psum | solution.py:31
  325.5 2.5 divide_convert_fusion
  328.0 0.1 copy.14
  328.1 2.1 all_gather.7
  330.3 2.0 copy.15
  332.3 2.0 copy.16
  334.3 0.0 copy-done
  334.3 5.1 %convolution_convert_fusion = bf16[896,4096]{1,0:T(8,128)(2,1)} fusion(bf16[896,256]{1,0:T(8,128)(2,1)S(1)} %all_gather.7, bf16[4096,256]{0,1:T(8,128)(2,1)S(1)} %copy-done), kind=kOutput, calls=%fused_computation.1 | convolution fusion | flops 1882718208 | bytes 9895936 | tf_op jit(solution)/shard_map/dot_general | solution.py:36
Async XLA Ops:
  7.2 67.0 %all-gather.2.cloned.1.call-start = ((), (), s32[]{:S(2)}) async-start(), calls=%async_computation | async-start | bytes 2228224 | tf_op jit(solution)/shard_map/all_gather | solution.py:24
  7.9 317.6 %all-reduce.3.cloned.1.call-start = ((), (), s32[]{:S(2)}) async-start(), calls=%async_computation.1 | async-start | bytes 14680064 | tf_op jit(solution)/shard_map/psum | solution.py:31
  94.3 1.0 copy-start.1
  94.3 239.9 %copy-start = (bf16[4096,256]{0,1:T(8,128)(2,1)S(1)}, bf16[4096,256]{0,1:T(8,128)(2,1)}, u32[]{:S(2)}) copy-start(bf16[4096,256]{0,1:T(8,128)(2,1)} %all-gather.2.cloned.1.call-done) | copy-start | bytes 6291460
Sparse Core Ops, SparseCore 0:
  10.8 63.3 all-gather.1
  94.5 230.9 all-reduce.2
where the time goes:
time: 347 us; the launch traced here: 346 us
  waiting for transfers between devices  296 us (85%)
  matrix products  19.7 us (6%)
  between operations  14.1 us (4%)
  blocking collectives  7.65 us (2%)
  local copies, waits for them, and re-layouts  6.52 us (2%)
    psum x1, waiting for transfers between devices, local(): block_total = lax.psum(block_terms, 'dp')  229 us
    all_gather x1, waiting for transfers between devices, local(): full_basis = lax.all_gather(projector, 'dp', axis=1, tiled=True)  66.3 us
    dot_general x1, matrix products, local(): lax.dot_general(grad_out, projected, (((0,), (0,)), ((), ())), preferred_...  9.35 us
  transfers between devices with their start and end apart: 2, of which 2 were waited for; matrix products, arithmetic and copies ran while one was open for 0% of the time, Pallas kernels for 0%

commit v1 on v0

v1 whole, which is shorter than its diff:
```python
import functools
import math

import jax
import jax.numpy as jnp
from jax import lax
from jax.experimental import pallas as pl
from jax.experimental.pallas import tpu as pltpu
from jax.sharding import PartitionSpec as P

STEP = 10


BETA_FIRST = 0.9
BETA_SECOND = 0.999
EPSILON = 1e-08


def adam_direction(grad_sub, moment, second):
    moment_new = BETA_FIRST * moment + (1.0 - BETA_FIRST) * grad_sub
    second_new = BETA_SECOND * second + (1.0 - BETA_SECOND) * grad_sub * grad_sub
    first_hat = moment_new / (1.0 - BETA_FIRST**STEP)
    second_hat = second_new / (1.0 - BETA_SECOND**STEP)
    direction = (first_hat / (jnp.sqrt(second_hat) + EPSILON)).astype(jnp.bfloat16)
    return (moment_new, second_new, direction)


def swap(block, axis, bit):
    size = lax.axis_size(axis)
    return lax.ppermute(block, axis, [(i, i ^ (1 << bit)) for i in range(size)])


def bit_of(index, bit):
    return (index >> bit) & 1


PHASES = ((0, 1, 2), (2, 0, 1), (1, 2, 0))
CHAINS = ((0, 1, 2, 3), (1, 2, 0, 3), (2, 0, 1, 3))
GATHERS = ((3, 1, 2, 0), (3, 2, 0, 1), (3, 0, 1, 2))


def column_parts(features):
    first = round(0.34 * features / 128) * 128
    return first, features - 2 * first, first


def row_parts(owned):
    first = round(0.32 * owned / 16) * 16
    return first, first, owned - 2 * first


def share(length, unit):
    units = length // unit
    ends = [(units * (p + 1) + 1) // 3 * unit for p in range(3)]
    return ends[0], ends[1] - ends[0], length - ends[1]


def swap_all(blocks, steps):
    return lax.optimization_barrier(
        [swap(block, "dp", bit) for block, bit in zip(blocks, steps)]
    )


def joined(held, other, bit, bits):
    first = bit_of(lax.axis_index("dp"), bit) == 0
    low = jnp.where(first, held, other)
    high = jnp.where(first, other, held)
    return jnp.concatenate([low, high], axis=bits - 1 - bit)


def gather_basis(columns, bits):
    rows, features = columns.shape
    whole = columns.reshape((1,) * bits + (rows, features))
    for bit in range(bits - 1, 2, -1):
        (other,) = swap_all([whole], [bit])
        whole = joined(whole, other, bit, bits)
    parts, start = [], 0
    for length in share(features, math.gcd(features, 128)):
        parts.append(whole[..., start : start + length])
        start += length
    for steps in PHASES[::-1]:
        others = swap_all(parts, steps)
        parts = [joined(h, o, bit, bits) for h, o, bit in zip(parts, others, steps)]
    return jnp.concatenate([part.reshape(-1, part.shape[-1]) for part in parts], axis=1)


def split(total, bit, bits):
    axis = bits - 1 - bit
    mine = bit_of(lax.axis_index("dp"), bit)
    kept = lax.dynamic_slice_in_dim(total, mine, 1, axis)
    given = lax.dynamic_slice_in_dim(total, 1 - mine, 1, axis).astype(jnp.bfloat16)
    return kept, given


def halved_all(pairs, steps):
    others = swap_all([given for _, given in pairs], steps)
    return [
        kept.astype(jnp.float32) + other.astype(jnp.float32)
        for (kept, _), other in zip(pairs, others)
    ]


VMEM = pl.BlockSpec(memory_space=pltpu.VMEM)
HBM = pl.BlockSpec(memory_space=pltpu.HBM)
MIB = 1024 * 1024
LIMIT = pltpu.CompilerParams(vmem_limit_bytes=16 * MIB)
TURN_LIMITS = [pltpu.CompilerParams(vmem_limit_bytes=size * MIB) for size in (48, 44)]


def bit_here(bit):
    return bit_of(lax.axis_index("dp"), bit)


def remaining(gone, bits):
    return [bit for bit in range(bits) if bit not in gone]


def gathered_kernels(columns, bits, turn):
    lengths = column_parts(columns.shape[1])
    whole = columns.reshape((1,) + columns.shape)
    other = swap(whole, "dp", 3)
    whole, other, early = lax.optimization_barrier((own(whole), other, turn(0)))
    held = list(join([whole], [other], [0], [3], lengths))
    others, places = [None] * 3, [None] * 3
    for part, order in enumerate(GATHERS):
        have = [3]
        for number, bit in enumerate(order[1:]):
            others[part] = swap(held[part], "dp", bit)
            have = sorted(have + [bit])
            places[part] = have.index(bit)
            if number < 2:
                (held[part],) = join([held[part]], [others[part]], [places[part]], [bit], None)
    others[0], late = lax.optimization_barrier((others[0], turn(1)))
    return list(zip(held, others, places, [order[3] for order in GATHERS])), [*early, *late]


def own_kernel(block_ref, out_ref):
    out_ref[...] = block_ref[...]


def own(block):
    return pl.pallas_call(
        own_kernel,
        out_shape=jax.ShapeDtypeStruct(block.shape, block.dtype),
        in_specs=[VMEM],
        out_specs=VMEM,
        compiler_params=LIMIT,
        name="own",
    )(block)


def join_kernel(places, bits, cut, *refs):
    count = len(places)
    held, other, outs = refs[:count], refs[count : 2 * count], refs[2 * count :]
    for part, (place, bit) in enumerate(zip(places, bits)):
        mine = bit_here(bit)
        low = 1 << place
        for index in range(held[part].shape[0]):
            base = (index // low) * 2 * low + index % low
            for source, side in ((held[part], mine), (other[part], 1 - mine)):
                if cut is None:
                    outs[part][base + side * low] = source[index]
                else:
                    start = 0
                    for out, length in zip(outs, cut):
                        out[base + side * low] = source[index, :, start : start + length]
                        start += length


def join(held, others, places, bits, cut):
    shapes = [(2 * x.shape[0],) + x.shape[1:] for x in held]
    if cut:
        shapes = [shapes[0][:-1] + (length,) for length in cut]
    return pl.pallas_call(
        functools.partial(join_kernel, places, bits, cut),
        out_shape=[jax.ShapeDtypeStruct(shape, jnp.bfloat16) for shape in shapes],
        in_specs=[VMEM] * (2 * len(held)),
        out_specs=[VMEM] * len(shapes),
        compiler_params=LIMIT,
        name="join",
    )(*held, *others)


def project_kernel(steps, starts, more, last, inputs_ref, *refs):
    count = len(steps)
    ends, refs = refs[: 2 * count], refs[2 * count :]
    (total_ref, *refs) = refs if more else (None, *refs)
    bases, outs = refs[:count], refs[count:]
    total = total_ref[...] if more else None
    for part, (place, bit) in enumerate(steps):
        held, other, basis = ends[2 * part], ends[2 * part + 1], bases[part]
        mine = bit_here(bit)
        low = 1 << place
        ranks, rows, length = held.shape
        for index in range(ranks):
            base = (index // low) * 2 * low + index % low
            basis[base + mine * low] = held[index]
            basis[base + (1 - mine) * low] = other[index]
        product = lax.dot_general(
            inputs_ref[:, starts[part] : starts[part] + length],
            basis[...].reshape(2 * ranks * rows, length),
            (((1,), (1,)), ((), ())),
            preferred_element_type=jnp.float32,
        )
        total = product if total is None else total + product
    outs[0][...] = total
    if last:
        outs[1][...] = total.astype(jnp.bfloat16)


def project(inputs, ends, starts, total, last):
    tokens = inputs.shape[0]
    operands, steps, shapes = [inputs], [], []
    for held, other, place, bit in ends:
        operands += [held, other]
        steps.append((place, bit))
        ranks, rows, length = held.shape
        shapes.append(jax.ShapeDtypeStruct((2 * ranks, rows, length), jnp.bfloat16))
    more = total is not None
    shapes.append(jax.ShapeDtypeStruct((tokens, 2 * ranks * rows), jnp.float32))
    if more:
        operands.append(total)
    if last:
        shapes.append(jax.ShapeDtypeStruct((tokens, 2 * ranks * rows), jnp.bfloat16))
    return pl.pallas_call(
        functools.partial(project_kernel, steps, starts, more, last),
        out_shape=shapes,
        in_specs=[VMEM] * len(operands),
        out_specs=[VMEM] * len(shapes),
        compiler_params=LIMIT,
        name="project",
    )(*operands)


def turn_kernel(half, lengths, owned, grad_ref, *refs):
    outs, (block, sems) = refs[:3], refs[3:]
    slots = block.shape[0]
    width = 2 * owned
    steps = grad_ref.shape[1] // width // 2
    first = half * steps

    def copy(step):
        columns = slice((first + step) * width, (first + step + 1) * width)
        slot = step % slots
        return pltpu.make_async_copy(
            grad_ref.at[:, columns], block.at[slot], sems.at[slot]
        )

    for step in range(slots):
        copy(step).start()
    for step in range(steps):
        copy(step).wait()
        rows = block[step % slots].T
        quarter, y = step // 2, step % 2
        for x in range(2):
            start = x * owned
            for part, length in enumerate(lengths):
                place = 2 * x + y if part == 0 else 2 * y + x
                outs[part][4 * quarter + place] = rows[start : start + length]
                start += length
        if step + slots < steps:
            copy(step + slots).start()


def turned_rows(grad_out, lengths, owned, half):
    tokens, units = grad_out.shape
    ranks = units // owned // 2
    return pl.pallas_call(
        functools.partial(turn_kernel, half, lengths, owned),
        out_shape=[
            jax.ShapeDtypeStruct((ranks, length, tokens), jnp.bfloat16) for length in lengths
        ],
        in_specs=[HBM],
        out_specs=[VMEM] * 3,
        scratch_shapes=[
            pltpu.VMEM((3, tokens, 2 * owned), jnp.bfloat16),
            pltpu.SemaphoreType.DMA((3,)),
        ],
        compiler_params=TURN_LIMITS[half],
        cost_estimate=pl.CostEstimate(
            flops=0, bytes_accessed=2 * tokens * units, transcendentals=0
        ),
        name="turn",
    )(grad_out)


def multiply(turned, projected, outs, stays):
    def write(out, first, block):
        count, length, tokens = block.shape
        terms = jnp.dot(
            block.reshape(-1, tokens), projected[...], preferred_element_type=jnp.float32
        )
        out[first : first + count] = terms.astype(out.dtype).reshape(count, length, -1)

    for part, out in outs.items():
        side = bit_here(CHAINS[part][0])
        side = side if stays else 1 - side
        if part < 2:
            for quarter in range(4):
                place = 4 * (quarter % 2) + 2 * side
                write(out, 2 * quarter, turned[quarter // 2][part][pl.ds(place, 2)])
        else:
            for far in range(2):
                write(out, 4 * far, turned[far][part][pl.ds(4 * side, 4)])


def first_kernel(part_ref, other_ref, *refs):
    turned, out, projected = (refs[:3], refs[3:6]), refs[6], refs[7]
    total = part_ref[...] + other_ref[...].astype(jnp.float32)
    projected[...] = total.astype(jnp.bfloat16)
    multiply(turned, projected, {2: out}, False)


def terms_kernel(parts, stays, projected, *refs):
    turned, outs = (refs[:3], refs[3:6]), refs[6:]
    multiply(turned, projected, dict(zip(parts, outs)), stays)


def terms_of(turned, lengths, operands, parts, stays):
    tokens, rank = operands[-1].shape
    kind = jnp.float32 if stays else jnp.bfloat16
    shapes = [jax.ShapeDtypeStruct((8, lengths[part], rank), kind) for part in parts]
    kernel = functools.partial(terms_kernel, parts, stays)
    if len(operands) == 2:
        kernel = first_kernel
        shapes.append(jax.ShapeDtypeStruct((tokens, rank), jnp.bfloat16))
    units = 8 * sum(lengths[part] for part in parts)
    return pl.pallas_call(
        kernel,
        out_shape=shapes,
        in_specs=[VMEM] * (len(operands) + 6),
        out_specs=[VMEM] * len(shapes),
        compiler_params=LIMIT,
        cost_estimate=pl.CostEstimate(
            flops=2 * tokens * units * rank,
            bytes_accessed=2 * units * tokens,
            transcendentals=0,
        ),
        name="kept_terms" if stays else "sent_terms",
    )(*operands, *turned)


def fold_kernel(place, bit, *refs):
    count = (len(refs) - 2) // 2
    kept, got, (stay, go) = refs[:count], refs[count : 2 * count], refs[2 * count :]
    mine = bit_here(bit)
    low = 1 << place
    start = 0
    for part in range(count):
        rows = slice(start, start + kept[part].shape[1])
        for index in range(stay.shape[0]):
            base = (index // low) * 2 * low + index % low
            here = base + mine * low
            there = base + (1 - mine) * low
            stay[index, rows] = kept[part][here] + got[part][here].astype(jnp.float32)
            total = kept[part][there] + got[part][there].astype(jnp.float32)
            go[index, rows] = total.astype(jnp.bfloat16)
        start = rows.stop


def fold(kept, got, place, bit):
    ranks, _, rank = kept[0].shape
    half = (ranks // 2, sum(x.shape[1] for x in kept), rank)
    return pl.pallas_call(
        functools.partial(fold_kernel, place, bit),
        out_shape=[
            jax.ShapeDtypeStruct(half, jnp.float32),
            jax.ShapeDtypeStruct(half, jnp.bfloat16),
        ],
        in_specs=[VMEM] * (2 * len(kept)),
        out_specs=[VMEM] * 2,
        compiler_params=LIMIT,
        name="fold",
    )(*kept, *got)


def adam_kernel(start, kept_ref, got_ref, moment_ref, second_ref, first, second, way):
    rows = pl.ds(start, first.shape[0])
    grad_sub = kept_ref[...] + got_ref[...].astype(jnp.float32)
    first[...], second[...], way[...] = adam_direction(
        grad_sub.reshape(first.shape), moment_ref[rows], second_ref[rows]
    )


def adam(kept, got, moment, second, start):
    shape = kept.shape[-2:]
    return pl.pallas_call(
        functools.partial(adam_kernel, start),
        out_shape=[
            jax.ShapeDtypeStruct(shape, jnp.float32),
            jax.ShapeDtypeStruct(shape, jnp.float32),
            jax.ShapeDtypeStruct(shape, jnp.bfloat16),
        ],
        in_specs=[VMEM] * 4,
        out_specs=[VMEM] * 3,
        compiler_params=LIMIT,
        name="adam",
    )(kept, got, moment, second)


def columns_of(bases):
    pieces, start = [], 0
    for part, basis in enumerate(bases):
        length = basis.shape[1]
        for first in range(0, length, 512):
            end = min(first + 512, length)
            pieces.append((part, first, slice(start + first, start + end)))
        start += length
    return pieces


def decode_kernel(nears, start, moments, holds, *refs):
    count = len(nears)
    directions, refs = refs[:count], refs[count:]
    bases, refs = refs[:3], refs[3:]
    pieces = refs[:moments]
    outs = refs[moments + holds :][: 1 + moments]
    block, sems, moment_sems = refs[-3:]
    here = pl.ds(start, block.shape[1])
    core = lax.axis_index("fsdp")
    copies = []
    for number, piece in enumerate(pieces):
        copies.append(
            pltpu.make_async_copy(piece, outs[1 + number].at[here], moment_sems.at[number])
        )
        copies[-1].start()
    for number, near in enumerate(nears):
        side = core if near else 1 - core
        for piece, (part, first, columns) in enumerate(columns_of(bases)):
            width = columns.stop - columns.start
            decoded = jnp.dot(
                directions[number][...],
                bases[part][:, first : first + width],
                preferred_element_type=jnp.float32,
            )
            block[number, :, columns] = decoded.astype(jnp.bfloat16)
            copies.append(
                pltpu.make_async_copy(
                    block.at[number, :, columns],
                    outs[0].at[side, here, columns],
                    sems.at[number, piece],
                )
            )
            copies[-1].start()
    for copy in copies:
        copy.wait()


def decode(directions, nears, bases, start, owned, pieces, held):
    rows, rank = directions[0].shape
    features = sum(basis.shape[1] for basis in bases)
    whole = jax.ShapeDtypeStruct((owned, rank), jnp.float32)
    shapes = [jax.ShapeDtypeStruct((2, owned, features), jnp.bfloat16)]
    shapes += [whole] * len(pieces)
    count = len(directions)
    given = count + len(bases) + len(pieces)
    return pl.pallas_call(
        functools.partial(decode_kernel, nears, start, len(pieces), len(held)),
        out_shape=shapes,
        in_specs=[VMEM] * given + [HBM] * len(held),
        out_specs=[HBM] * len(shapes),
        scratch_shapes=[
            pltpu.VMEM((count, rows, features), jnp.bfloat16),
            pltpu.SemaphoreType.DMA((count, len(columns_of(bases)))),
            pltpu.SemaphoreType.DMA((2,)),
        ],
        input_output_aliases={given + i: i for i in range(len(held))},
        compiler_params=LIMIT,
        name="decode",
    )(*directions, *bases, *pieces, *held)


def exchanged(kept, got, order, number):
    bit = order[number]
    place = remaining(order[:number], len(order)).index(bit)
    stay, go = fold(kept, got, place, bit)
    return stay, swap(go, "dp", bit)


def sum_in_kernels(turned, part, other, lengths):
    last, projected = terms_of(turned, lengths, (part, other), (2,), False)
    far = swap(last, "dp", CHAINS[2][0])
    sent = terms_of(turned, lengths, (projected,), (0, 1), False)
    got = [swap(x, "dp", order[0]) for x, order in zip(sent, CHAINS)]
    got.append(far)
    kept = terms_of(turned, lengths, (projected,), (0, 1, 2), True)
    pairs = list(zip(kept, got))
    for number in range(1, 4):
        for p, order in enumerate(CHAINS):
            if p == 2 or number < 3:
                kept, got = pairs[p]
                pairs[p] = exchanged([kept], [got], order, number)
    both = exchanged(*zip(*pairs[:2]), CHAINS[0], 3)
    return both, pairs[2]


def plain_terms(grad_out, projected, lengths, owned, bits):
    terms = lax.dot_general(
        grad_out, projected, (((0,), (0,)), ((), ())), preferred_element_type=jnp.float32
    )
    terms = terms.reshape((2,) * bits + (owned, -1))
    pairs, start = [], 0
    for bit, length in enumerate(lengths):
        pairs.append(split(terms[..., start : start + length, :], bit, bits))
        start += length
    return pairs


def sum_rows(pairs, lengths, bits):
    shaped = []
    for bit, (length, pair) in enumerate(zip(lengths, pairs)):
        shape = [2] * bits
        shape[bits - 1 - bit] = 1
        shaped.append([x.reshape(tuple(shape) + (length, -1)) for x in pair])
    sums = halved_all(shaped, PHASES[0])
    for steps in PHASES[1:]:
        sums = halved_all([split(x, bit, bits) for x, bit in zip(sums, steps)], steps)
    total = jnp.concatenate(sums, axis=bits)
    for bit in range(3, bits):
        (total,) = halved_all([split(total, bit, bits)], [bit])
    return total.reshape(-1, total.shape[-1])


def exchange(block):
    return swap(block, "fsdp", 0)


def kernel_local(inputs, grad_out, projector, moment, second):
    ranks = lax.axis_size("dp")
    bits = ranks.bit_length() - 1
    owned = grad_out.shape[1] // ranks
    lengths = row_parts(owned)

    def turn(half):
        return turned_rows(grad_out, lengths, owned, half)

    ends, turned = gathered_kernels(projector.T, bits, turn)
    widths = [end[0].shape[2] for end in ends]
    starts = [0, widths[0], widths[0] + widths[1]]
    left, total = project(inputs, [ends[0]], [starts[0]], None, False)
    right, total = project(inputs, [ends[2]], [starts[2]], total, False)
    middle, part, sent = project(inputs, [ends[1]], [starts[1]], total, True)
    bases = [x.reshape(-1, x.shape[2]) for x in (left, middle, right)]
    other = exchange(sent)
    both, last = sum_in_kernels(turned, part, other, lengths)
    held = []
    start = lengths[0] + lengths[1]
    *pieces, direction = adam(*last, moment, second, start)
    far = exchange(direction)
    held = decode([direction], [True], bases, start, owned, pieces, held)
    far, held = lax.optimization_barrier((far, held))
    update, *moments = held
    (update,) = decode([far], [False], bases, start, owned, [], [update])
    held = [update, *moments]
    both, held = lax.optimization_barrier((both, held))
    *pieces, direction = adam(*both, moment, second, 0)
    far = exchange(direction)
    held = decode([direction], [True], bases, 0, owned, pieces, held)
    far, held = lax.optimization_barrier((far, held))
    update, *moments = held
    (update,) = decode([far], [False], bases, 0, owned, [], [update])
    return (update, *moments)


def plain_local(inputs, grad_out, projector, moment, second):
    ranks = lax.axis_size("dp")
    bits = ranks.bit_length() - 1
    basis = gather_basis(projector.T, bits)
    part = lax.dot_general(
        inputs, basis, (((1,), (1,)), ((), ())), preferred_element_type=jnp.float32
    )
    projected = lax.psum(part, "fsdp").astype(jnp.bfloat16)
    owned = grad_out.shape[1] // ranks
    lengths = share(owned, math.gcd(owned, 16))
    pairs = plain_terms(grad_out, projected, lengths, owned, bits)
    grad_sub = sum_rows(pairs, lengths, bits)
    moment_new, second_new, direction = adam_direction(grad_sub, moment, second)
    gathered = lax.all_gather(direction, "fsdp", axis=0, tiled=True)
    decoded = lax.dot_general(
        gathered, basis, (((1,), (0,)), ((), ())), preferred_element_type=jnp.float32
    )
    blocks = lax.axis_size("fsdp")
    update = decoded.astype(jnp.bfloat16).reshape(blocks, owned, decoded.shape[1])
    return (update, moment_new, second_new)


def local(inputs, grad_out, projector, moment, second):
    owned = grad_out.shape[1] // lax.axis_size("dp")
    fits = lax.axis_size("fsdp") == 2 and lax.axis_size("dp") == 16 and owned % 64 == 0
    run = kernel_local if fits else plain_local
    return run(inputs, grad_out, projector, moment, second)


def solution(mesh):
    return jax.shard_map(
        local,
        mesh=mesh,
        in_specs=(
            P("dp", "fsdp"),
            P("dp", "fsdp"),
            P("fsdp", "dp"),
            P(("fsdp", "dp"), None),
            P(("fsdp", "dp"), None),
        ),
        out_specs=(P(None, "dp", "fsdp"), P(("fsdp", "dp"), None), P(("fsdp", "dp"), None)),
        check_vma=False,
    )
```

time: 347 us -> 86.9 us (0.25)
  waiting for transfers between devices: 296 us -> 36.2 us
  starting transfers between devices: 0.08 us -> 27.4 us
  Pallas kernels: 0 us -> 21.3 us
  matrix products: 19.7 us -> 0 us
  between operations: 14.1 us -> 0.87 us
  blocking collectives: 7.65 us -> 0 us
  local copies, waits for them, and re-layouts: 6.52 us -> 0.96 us
    psum x1 -> x0, waiting for transfers between devices: 229 us -> none  [local(): block_total = lax.psum(block_terms, 'dp')]
    all_gather x1 -> x0, waiting for transfers between devices: 66.3 us -> none  [local(): full_basis = lax.all_gather(projector, 'dp', axis=1, tiled=True)]
    ppermute x0 -> x24, waiting for transfers between devices: none -> 36.2 us  [swap(): return lax.ppermute(block, axis, [(i, i ^ 1 << bit) for i in range(size)])]
    ppermute x0 -> x24, starting transfers between devices: none -> 27.4 us  [swap(): return lax.ppermute(block, axis, [(i, i ^ 1 << bit) for i in range(size)])]
    pallas_call x0 -> x30, Pallas kernels: none -> 21.3 us  [the longest x2 7.89 us: turned_rows(): pl.pallas_call(functools.partial(turn_kernel, half, lengths, owned), out_...]
    dot_general x3 -> x0, matrix products: 19.7 us -> none  [the longest x1 9.35 us: local(): lax.dot_general(grad_out, projected, (((0,), (0,)), ((), ())), preferred_...]
    psum x1 -> x0, blocking collectives: 5.51 us -> none  [local(): projected = lax.psum(local_proj, 'fsdp').astype(jnp.bfloat16)]
    unnamed x8 -> x10, local copies, waits for them, and re-layouts: 6.39 us -> 0.96 us
  transfers between devices with their start and end apart: 2 -> 24, of which waited for: 2 -> 12; matrix products, arithmetic and copies ran while one was open for 0% -> 0% of each run, Pallas kernels for 0% -> 20%
where the time goes in v1:
time: 86.9 us; the launch traced here: 86.7 us
  waiting for transfers between devices  36.2 us (42%)
  starting transfers between devices  27.4 us (32%)
  Pallas kernels  21.3 us (25%)
  local copies, waits for them, and re-layouts  0.96 us (1%)
  between operations  0.87 us (1%)
    ppermute x24, waiting for transfers between devices, swap(): return lax.ppermute(block, axis, [(i, i ^ 1 << bit) for i in range(size)])  36.2 us
    ppermute x24, starting transfers between devices, swap(): return lax.ppermute(block, axis, [(i, i ^ 1 << bit) for i in range(size)])  27.4 us
    pallas_call x2, Pallas kernels, turned_rows(): pl.pallas_call(functools.partial(turn_kernel, half, lengths, owned), out_...  7.89 us
    pallas_call x4, Pallas kernels, decode(): pl.pallas_call(functools.partial(decode_kernel, nears, start, len(pieces)...  6.4 us
    pallas_call x3, Pallas kernels, terms_of(): pl.pallas_call(kernel, out_shape=shapes, in_specs=[VMEM] * (len(operands)...  3.33 us
    pallas_call x3, Pallas kernels, project(): pl.pallas_call(functools.partial(project_kernel, steps, starts, more, las...  2.42 us
  transfers between devices with their start and end apart: 24, of which 12 were waited for; matrix products, arithmetic and copies ran while one was open for 0% of the time, Pallas kernels for 20%

profile of v1, /device:TPU:0, one launch (start us, length us, event | category | flops | bytes accessed | tf_op | source)
XLA Modules:
  0.0 86.7 jit_solution(8128380112103107963)
XLA Ops:
  0.6 4.1 %collective-permute-start = (bf16[1,16,4096]{2,1,0:T(8,128)(2,1)}, bf16[1,16,4096]{2,1,0:T(8,128)(2,1)S(1)}, u32[]{:S(2)}, u32[]{:S(2)}) collective-permute-start(bf16[1,16,4096]{2,1,0:T(8,128)(2,1)} %bitcast.20), channel_id=1, source_target_pairs={{0,16},{2,18},{4,20},{6,22},{8,24},{10,26},{12,28},{14,30},{16,0},... | collective-permute-start | bytes 393224 | tf_op jit(solution)/shard_map/ppermute | solution.py:30
  5.7 3.6 %turn.2 = (bf16[8,144,768]{2,1,0:T(8,128)(2,1)S(1)}, bf16[8,144,768]{2,1,0:T(8,128)(2,1)S(1)}, bf16[8,160,768]{2,1,0:T(8,128)(2,1)S(1)}) custom-call(bf16[768,7168]{1,0:T(8,128)(2,1)} %grad_ref.3), custom_call_target="tpu_custom_call" | custom-call | bytes 11010048 | tf_op jit(solution)/shard_map/turn/pallas_call | solution.py:268
  9.3 2.0 %collective-permute-done.refs_1_ = bf16[1,16,4096]{2,1,0:T(8,128)(2,1)S(1)} collective-permute-done((bf16[1,16,4096]{2,1,0:T(8,128)(2,1)}, bf16[1,16,4096]{2,1,0:T(8,128)(2,1)S(1)}, u32[]{:S(2)}, u32[]{:S(2)}) %collective-permute-start) | collective-permute-done | bytes 131104 | tf_op jit(solution)/shard_map/ppermute | solution.py:30
  11.3 1.6 %collective-permute-start.7 = (bf16[2,16,1408]{2,1,0:T(8,128)(2,1)S(1)}, bf16[2,16,1408]{2,1,0:T(8,128)(2,1)S(1)}, u32[]{:S(2)}, u32[]{:S(2)}) collective-permute-start(bf16[2,16,1408]{2,1,0:T(8,128)(2,1)S(1)} %get-tuple-element.83.refs_0_), channel_id=1, source_target_pairs={{0,4},{2,6},{4,0},{6,2},{8,12},{10,14},{12,8},{14,10},{16,20},{18,... | collective-permute-start | bytes 270344 | tf_op jit(solution)/shard_map/ppermute | solution.py:30
  12.9 1.5 %collective-permute-start.4 = (bf16[2,16,1408]{2,1,0:T(8,128)(2,1)S(1)}, bf16[2,16,1408]{2,1,0:T(8,128)(2,1)S(1)}, u32[]{:S(2)}, u32[]{:S(2)}) collective-permute-start(bf16[2,16,1408]{2,1,0:T(8,128)(2,1)S(1)} %get-tuple-element.82.refs_0_), channel_id=1, source_target_pairs={{0,2},{2,0},{4,6},{6,4},{8,10},{10,8},{12,14},{14,12},{16,18},{18,... | collective-permute-start | bytes 270344 | tf_op jit(solution)/shard_map/ppermute | solution.py:30
  18.4 1.3 %collective-permute-done.1.refs_1_ = bf16[2,16,1280]{2,1,0:T(8,128)(2,1)S(1)} collective-permute-done((bf16[2,16,1280]{2,1,0:T(8,128)(2,1)S(1)}, bf16[2,16,1280]{2,1,0:T(8,128)(2,1)S(1)}, u32[]{:S(2)}, u32[]{:S(2)}) %collective-permute-start.1) | collective-permute-done | bytes 81952 | tf_op jit(solution)/shard_map/ppermute | solution.py:30
  20.4 1.4 %collective-permute-done.8.refs_1_ = bf16[4,16,1408]{2,1,0:T(8,128)(2,1)S(1)} collective-permute-done((bf16[4,16,1408]{2,1,0:T(8,128)(2,1)S(1)}, bf16[4,16,1408]{2,1,0:T(8,128)(2,1)S(1)}, u32[]{:S(2)}, u32[]{:S(2)}) %collective-permute-start.8) | collective-permute-done | bytes 180256 | tf_op jit(solution)/shard_map/ppermute | solution.py:30
  21.8 1.3 %collective-permute-start.9 = (bf16[8,16,1408]{2,1,0:T(8,128)(2,1)S(1)}, bf16[8,16,1408]{2,1,0:T(8,128)(2,1)S(1)}, u32[]{:S(2)}, u32[]{:S(2)}) collective-permute-start(bf16[8,16,1408]{2,1,0:T(8,128)(2,1)S(1)} %join.13.refs_0_), channel_id=1, source_target_pairs={{0,2},{2,0},{4,6},{6,4},{8,10},{10,8},{12,14},{14,12},{16,18},{18,... | collective-permute-start | bytes 1081352 | tf_op jit(solution)/shard_map/ppermute | solution.py:30
  24.2 2.6 %collective-permute-done.2.refs_1_ = bf16[4,16,1280]{2,1,0:T(8,128)(2,1)S(1)} collective-permute-done((bf16[4,16,1280]{2,1,0:T(8,128)(2,1)S(1)}, bf16[4,16,1280]{2,1,0:T(8,128)(2,1)S(1)}, u32[]{:S(2)}, u32[]{:S(2)}) %collective-permute-start.2) | collective-permute-done | bytes 163872 | tf_op jit(solution)/shard_map/ppermute | solution.py:30
  27.5 4.3 %turn.3 = (bf16[8,144,768]{2,1,0:T(8,128)(2,1)S(1)}, bf16[8,144,768]{2,1,0:T(8,128)(2,1)S(1)}, bf16[8,160,768]{2,1,0:T(8,128)(2,1)S(1)}) custom-call(bf16[768,7168]{1,0:T(8,128)(2,1)} %grad_ref.3), custom_call_target="tpu_custom_call" | custom-call | bytes 11010048 | tf_op jit(solution)/shard_map/turn/pallas_call | solution.py:268
  34.9 1.7 %collective-permute-done.10.other_ref = bf16[768,256]{1,0:T(8,128)(2,1)S(1)} collective-permute-done((bf16[768,256]{1,0:T(8,128)(2,1)S(1)}, bf16[768,256]{1,0:T(8,128)(2,1)S(1)}, u32[]{:S(2)}, u32[]{:S(2)}) %collective-permute-start.10) | collective-permute-done | bytes 393248 | tf_op jit(solution)/shard_map/ppermute | solution.py:30
  37.2 1.4 %collective-permute-start.18 = (bf16[8,160,256]{2,1,0:T(8,128)(2,1)S(1)}, bf16[8,160,256]{2,1,0:T(8,128)(2,1)S(1)}, u32[]{:S(2)}, u32[]{:S(2)}) collective-permute-start(bf16[8,160,256]{2,1,0:T(8,128)(2,1)S(1)} %get-tuple-element.114), channel_id=1, source_target_pairs={{0,8},{2,10},{4,12},{6,14},{8,0},{10,2},{12,4},{14,6},{16,24},{18,... | collective-permute-start | bytes 1966088 | tf_op jit(solution)/shard_map/ppermute | solution.py:30
  41.1 1.6 %kept_terms.1 = (f32[8,144,256]{2,1,0:T(8,128)S(1)}, f32[8,144,256]{2,1,0:T(8,128)S(1)}, f32[8,160,256]{2,1,0:T(8,128)S(1)}) custom-call(bf16[768,256]{1,0:T(8,128)(2,1)S(1)} %get-tuple-element.98.projected, bf16[8,144,768]{2,1,0:T(8,128)(2,1)S(1)} %get-tuple-element.92.refs_0_, bf16[8,144,768]{2,1,0:T(8,128)(2,1)S(1)} %get-tuple-element.93.refs_1_, ...), custom_call_target="tpu_custom_call" | custom-call | flops 1409286144 | bytes 5505024 | tf_op jit(solution)/shard_map/kept_terms/pallas_call | solution.py:328
  42.7 11.4 %collective-permute-done.18.refs_1_ = bf16[8,160,256]{2,1,0:T(8,128)(2,1)S(1)} collective-permute-done((bf16[8,160,256]{2,1,0:T(8,128)(2,1)S(1)}, bf16[8,160,256]{2,1,0:T(8,128)(2,1)S(1)}, u32[]{:S(2)}, u32[]{:S(2)}) %collective-permute-start.18) | collective-permute-done | bytes 655392 | tf_op jit(solution)/shard_map/ppermute | solution.py:30
  57.3 5.9 %collective-permute-done.19.refs_1_ = bf16[4,160,256]{2,1,0:T(8,128)(2,1)S(1)} collective-permute-done((bf16[4,160,256]{2,1,0:T(8,128)(2,1)S(1)}, bf16[4,160,256]{2,1,0:T(8,128)(2,1)S(1)}, u32[]{:S(2)}, u32[]{:S(2)}) %collective-permute-start.19) | collective-permute-done | bytes 327712 | tf_op jit(solution)/shard_map/ppermute | solution.py:30
  64.9 1.4 %collective-permute-start.16 = (bf16[2,144,256]{2,1,0:T(8,128)(2,1)S(1)}, bf16[2,144,256]{2,1,0:T(8,128)(2,1)S(1)}, u32[]{:S(2)}, u32[]{:S(2)}) collective-permute-start(bf16[2,144,256]{2,1,0:T(8,128)(2,1)S(1)} %get-tuple-element.110), channel_id=1, source_target_pairs={{0,2},{2,0},{4,6},{6,4},{8,10},{10,8},{12,14},{14,12},{16,18},{18,... | collective-permute-start | bytes 442376 | tf_op jit(solution)/shard_map/ppermute | solution.py:30
  66.2 2.4 %collective-permute-done.20.refs_1_ = bf16[2,160,256]{2,1,0:T(8,128)(2,1)S(1)} collective-permute-done((bf16[2,160,256]{2,1,0:T(8,128)(2,1)S(1)}, bf16[2,160,256]{2,1,0:T(8,128)(2,1)S(1)}, u32[]{:S(2)}, u32[]{:S(2)}) %collective-permute-start.20) | collective-permute-done | bytes 163872 | tf_op jit(solution)/shard_map/ppermute | solution.py:30
  68.7 3.2 %collective-permute-start.21 = (bf16[1,160,256]{2,1,0:T(8,128)(2,1)S(1)}, bf16[1,160,256]{2,1,0:T(8,128)(2,1)S(1)}, u32[]{:S(2)}, u32[]{:S(2)}) collective-permute-start(bf16[1,160,256]{2,1,0:T(8,128)(2,1)S(1)} %get-tuple-element.120), channel_id=1, source_target_pairs={{0,16},{2,18},{4,20},{6,22},{8,24},{10,26},{12,28},{14,30},{16,0},... | collective-permute-start | bytes 245768 | tf_op jit(solution)/shard_map/ppermute | solution.py:30
  72.0 1.5 %collective-permute-start.17 = (bf16[1,288,256]{2,1,0:T(8,128)(2,1)S(1)}, bf16[1,288,256]{2,1,0:T(8,128)(2,1)S(1)}, u32[]{:S(2)}, u32[]{:S(2)}) collective-permute-start(bf16[1,288,256]{2,1,0:T(8,128)(2,1)S(1)} %get-tuple-element.112), channel_id=1, source_target_pairs={{0,16},{2,18},{4,20},{6,22},{8,24},{10,26},{12,28},{14,30},{16,0},... | collective-permute-start | bytes 442376 | tf_op jit(solution)/shard_map/ppermute | solution.py:30
  73.5 5.7 %collective-permute-done.21.got_ref = bf16[1,160,256]{2,1,0:T(8,128)(2,1)S(1)} collective-permute-done((bf16[1,160,256]{2,1,0:T(8,128)(2,1)S(1)}, bf16[1,160,256]{2,1,0:T(8,128)(2,1)S(1)}, u32[]{:S(2)}, u32[]{:S(2)}) %collective-permute-start.21) | collective-permute-done | bytes 81952 | tf_op jit(solution)/shard_map/ppermute | solution.py:30
  79.4 1.4 %decode.4 = (bf16[2,448,4096]{2,1,0:T(8,128)(2,1)}, f32[448,256]{1,0:T(8,128)}, f32[448,256]{1,0:T(8,128)}) custom-call(bf16[160,256]{1,0:T(8,128)(2,1)S(1)} %get-tuple-element.121.refs_0_, bf16[256,1408]{1,0:T(8,128)(2,1)S(1)} %bitcast.8, bf16[256,1280]{1,0:T(8,128)(2,1)S(1)} %bitcast.16, bf16[256,1408]{1,0:T(8,128)(2,1)S(1)} %bitcast.12, ...), custom_call_target="tpu_custom_call" | custom-call | tf_op jit(solution)/shard_map/decode/pallas_call | solution.py:457
  80.8 1.4 %decode.5.refs_6_ = bf16[2,448,4096]{2,1,0:T(8,128)(2,1)} custom-call(bf16[160,256]{1,0:T(8,128)(2,1)S(1)} %collective-permute-done.22.refs_0_, bf16[256,1408]{1,0:T(8,128)(2,1)S(1)} %bitcast.9, bf16[256,1280]{1,0:T(8,128)(2,1)S(1)} %bitcast.17, bf16[256,1408]{1,0:T(8,128)(2,1)S(1)} %bitcast.13, ...), custom_call_target="tpu_custom_call", output_to_operand_aliasing={{}: (4, {})} | custom-call | tf_op jit(solution)/shard_map/decode/pallas_call | solution.py:457
  83.0 1.9 %decode.6 = (bf16[2,448,4096]{2,1,0:T(8,128)(2,1)}, f32[448,256]{1,0:T(8,128)}, f32[448,256]{1,0:T(8,128)}) custom-call(bf16[288,256]{1,0:T(8,128)(2,1)S(1)} %get-tuple-element.136.refs_0_, bf16[256,1408]{1,0:T(8,128)(2,1)S(1)} %bitcast.10, bf16[256,1280]{1,0:T(8,128)(2,1)S(1)} %bitcast.18, ...), custom_call_target="tpu_custom_call", output_to_operand_aliasing={{0}: (6, {}), {1}: (7, {}), {2}: (8, {})} | custom-call | tf_op jit(solution)/shard_map/decode/pallas_call | solution.py:457
  84.9 1.8 %decode.7 = bf16[2,448,4096]{2,1,0:T(8,128)(2,1)} custom-call(bf16[288,256]{1,0:T(8,128)(2,1)S(1)} %collective-permute-done.23.refs_0_, bf16[256,1408]{1,0:T(8,128)(2,1)S(1)} %bitcast.11, bf16[256,1280]{1,0:T(8,128)(2,1)S(1)} %bitcast.19, bf16[256,1408]{1,0:T(8,128)(2,1)S(1)} %bitcast.15, ...), custom_call_target="tpu_custom_call", output_to_operand_aliasing={{}: (4, {})} | custom-call | tf_op jit(solution)/shard_map/decode/pallas_call | solution.py:457
  (65 shorter events, 19.5 us)
Async XLA Ops:
  0.6 10.6 %collective-permute-start = (bf16[1,16,4096]{2,1,0:T(8,128)(2,1)}, bf16[1,16,4096]{2,1,0:T(8,128)(2,1)S(1)}, u32[]{:S(2)}, u32[]{:S(2)}) collective-permute-start(bf16[1,16,4096]{2,1,0:T(8,128)(2,1)} %bitcast.20), channel_id=1, source_target_pairs={{0,16},{2,18},{4,20},{6,22},{8,24},{10,26},{12,28},{14,30},{16,0},... | collective-permute-start | bytes 393224 | tf_op jit(solution)/shard_map/ppermute | solution.py:30
  11.3 4.6 %collective-permute-start.7 = (bf16[2,16,1408]{2,1,0:T(8,128)(2,1)S(1)}, bf16[2,16,1408]{2,1,0:T(8,128)(2,1)S(1)}, u32[]{:S(2)}, u32[]{:S(2)}) collective-permute-start(bf16[2,16,1408]{2,1,0:T(8,128)(2,1)S(1)} %get-tuple-element.83.refs_0_), channel_id=1, source_target_pairs={{0,4},{2,6},{4,0},{6,2},{8,12},{10,14},{12,8},{14,10},{16,20},{18,... | collective-permute-start | bytes 270344 | tf_op jit(solution)/shard_map/ppermute | solution.py:30
  12.9 4.5 %collective-permute-start.4 = (bf16[2,16,1408]{2,1,0:T(8,128)(2,1)S(1)}, bf16[2,16,1408]{2,1,0:T(8,128)(2,1)S(1)}, u32[]{:S(2)}, u32[]{:S(2)}) collective-permute-start(bf16[2,16,1408]{2,1,0:T(8,128)(2,1)S(1)} %get-tuple-element.82.refs_0_), channel_id=1, source_target_pairs={{0,2},{2,0},{4,6},{6,4},{8,10},{10,8},{12,14},{14,12},{16,18},{18,... | collective-permute-start | bytes 270344 | tf_op jit(solution)/shard_map/ppermute | solution.py:30
  14.4 5.3 %collective-permute-start.1 = (bf16[2,16,1280]{2,1,0:T(8,128)(2,1)S(1)}, bf16[2,16,1280]{2,1,0:T(8,128)(2,1)S(1)}, u32[]{:S(2)}, u32[]{:S(2)}) collective-permute-start(bf16[2,16,1280]{2,1,0:T(8,128)(2,1)S(1)} %get-tuple-element.81.refs_0_), channel_id=1, source_target_pairs={{0,8},{2,10},{4,12},{6,14},{8,0},{10,2},{12,4},{14,6},{16,24},{18,... | collective-permute-start | bytes 245768 | tf_op jit(solution)/shard_map/ppermute | solution.py:30
  15.9 5.9 %collective-permute-start.8 = (bf16[4,16,1408]{2,1,0:T(8,128)(2,1)S(1)}, bf16[4,16,1408]{2,1,0:T(8,128)(2,1)S(1)}, u32[]{:S(2)}, u32[]{:S(2)}) collective-permute-start(bf16[4,16,1408]{2,1,0:T(8,128)(2,1)S(1)} %join.12.refs_0_), channel_id=1, source_target_pairs={{0,8},{2,10},{4,12},{6,14},{8,0},{10,2},{12,4},{14,6},{16,24},{18,... | collective-permute-start | bytes 540680 | tf_op jit(solution)/shard_map/ppermute | solution.py:30
  17.5 5.7 %collective-permute-start.5 = (bf16[4,16,1408]{2,1,0:T(8,128)(2,1)S(1)}, bf16[4,16,1408]{2,1,0:T(8,128)(2,1)S(1)}, u32[]{:S(2)}, u32[]{:S(2)}) collective-permute-start(bf16[4,16,1408]{2,1,0:T(8,128)(2,1)S(1)} %join.10.refs_0_), channel_id=1, source_target_pairs={{0,4},{2,6},{4,0},{6,2},{8,12},{10,14},{12,8},{14,10},{16,20},{18,... | collective-permute-start | bytes 540680 | tf_op jit(solution)/shard_map/ppermute | solution.py:30
  19.7 7.1 %collective-permute-start.2 = (bf16[4,16,1280]{2,1,0:T(8,128)(2,1)S(1)}, bf16[4,16,1280]{2,1,0:T(8,128)(2,1)S(1)}, u32[]{:S(2)}, u32[]{:S(2)}) collective-permute-start(bf16[4,16,1280]{2,1,0:T(8,128)(2,1)S(1)} %join.8.refs_0_), channel_id=1, source_target_pairs={{0,2},{2,0},{4,6},{6,4},{8,10},{10,8},{12,14},{14,12},{16,18},{18,... | collective-permute-start | bytes 491528 | tf_op jit(solution)/shard_map/ppermute | solution.py:30
  21.8 10.5 %collective-permute-start.9 = (bf16[8,16,1408]{2,1,0:T(8,128)(2,1)S(1)}, bf16[8,16,1408]{2,1,0:T(8,128)(2,1)S(1)}, u32[]{:S(2)}, u32[]{:S(2)}) collective-permute-start(bf16[8,16,1408]{2,1,0:T(8,128)(2,1)S(1)} %join.13.refs_0_), channel_id=1, source_target_pairs={{0,2},{2,0},{4,6},{6,4},{8,10},{10,8},{12,14},{14,12},{16,18},{18,... | collective-permute-start | bytes 1081352 | tf_op jit(solution)/shard_map/ppermute | solution.py:30
  23.2 9.9 %collective-permute-start.6 = (bf16[8,16,1408]{2,1,0:T(8,128)(2,1)S(1)}, bf16[8,16,1408]{2,1,0:T(8,128)(2,1)S(1)}, u32[]{:S(2)}, u32[]{:S(2)}) collective-permute-start(bf16[8,16,1408]{2,1,0:T(8,128)(2,1)S(1)} %join.11.refs_0_), channel_id=1, source_target_pairs={{0,8},{2,10},{4,12},{6,14},{8,0},{10,2},{12,4},{14,6},{16,24},{18,... | collective-permute-start | bytes 1081352 | tf_op jit(solution)/shard_map/ppermute | solution.py:30
  26.9 7.2 %collective-permute-start.3 = (bf16[8,16,1280]{2,1,0:T(8,128)(2,1)S(1)}, bf16[8,16,1280]{2,1,0:T(8,128)(2,1)S(1)}, u32[]{:S(2)}, u32[]{:S(2)}) collective-permute-start(bf16[8,16,1280]{2,1,0:T(8,128)(2,1)S(1)} %join.9.refs_0_), channel_id=1, source_target_pairs={{0,4},{2,6},{4,0},{6,2},{8,12},{10,14},{12,8},{14,10},{16,20},{18,... | collective-permute-start | bytes 983048 | tf_op jit(solution)/shard_map/ppermute | solution.py:30
  34.8 1.8 %collective-permute-start.10 = (bf16[768,256]{1,0:T(8,128)(2,1)S(1)}, bf16[768,256]{1,0:T(8,128)(2,1)S(1)}, u32[]{:S(2)}, u32[]{:S(2)}) collective-permute-start(bf16[768,256]{1,0:T(8,128)(2,1)S(1)} %get-tuple-element.91), channel_id=1, source_target_pairs={{0,1},{1,0},{2,3},{3,2},{4,5},{5,4},{6,7},{7,6},{8,9},{9,8},{10,11... | collective-permute-start | bytes 1179656 | tf_op jit(solution)/shard_map/ppermute | solution.py:30
  37.2 16.8 %collective-permute-start.18 = (bf16[8,160,256]{2,1,0:T(8,128)(2,1)S(1)}, bf16[8,160,256]{2,1,0:T(8,128)(2,1)S(1)}, u32[]{:S(2)}, u32[]{:S(2)}) collective-permute-start(bf16[8,160,256]{2,1,0:T(8,128)(2,1)S(1)} %get-tuple-element.114), channel_id=1, source_target_pairs={{0,8},{2,10},{4,12},{6,14},{8,0},{10,2},{12,4},{14,6},{16,24},{18,... | collective-permute-start | bytes 1966088 | tf_op jit(solution)/shard_map/ppermute | solution.py:30
  39.7 15.4 %collective-permute-start.11 = (bf16[8,144,256]{2,1,0:T(8,128)(2,1)S(1)}, bf16[8,144,256]{2,1,0:T(8,128)(2,1)S(1)}, u32[]{:S(2)}, u32[]{:S(2)}) collective-permute-start(bf16[8,144,256]{2,1,0:T(8,128)(2,1)S(1)} %get-tuple-element.100), channel_id=1, source_target_pairs={{0,2},{2,0},{4,6},{6,4},{8,10},{10,8},{12,14},{14,12},{16,18},{18,... | collective-permute-start | bytes 1769480 | tf_op jit(solution)/shard_map/ppermute | solution.py:30
  40.5 15.5 %collective-permute-start.13 = (bf16[8,144,256]{2,1,0:T(8,128)(2,1)S(1)}, bf16[8,144,256]{2,1,0:T(8,128)(2,1)S(1)}, u32[]{:S(2)}, u32[]{:S(2)}) collective-permute-start(bf16[8,144,256]{2,1,0:T(8,128)(2,1)S(1)} %get-tuple-element.105), channel_id=1, source_target_pairs={{0,4},{2,6},{4,0},{6,2},{8,12},{10,14},{12,8},{14,10},{16,20},{18,... | collective-permute-start | bytes 1769480 | tf_op jit(solution)/shard_map/ppermute | solution.py:30
  54.2 9.0 %collective-permute-start.19 = (bf16[4,160,256]{2,1,0:T(8,128)(2,1)S(1)}, bf16[4,160,256]{2,1,0:T(8,128)(2,1)S(1)}, u32[]{:S(2)}, u32[]{:S(2)}) collective-permute-start(bf16[4,160,256]{2,1,0:T(8,128)(2,1)S(1)} %get-tuple-element.116), channel_id=1, source_target_pairs={{0,2},{2,0},{4,6},{6,4},{8,10},{10,8},{12,14},{14,12},{16,18},{18,... | collective-permute-start | bytes 983048 | tf_op jit(solution)/shard_map/ppermute | solution.py:30
  55.2 9.0 %collective-permute-start.12 = (bf16[4,144,256]{2,1,0:T(8,128)(2,1)S(1)}, bf16[4,144,256]{2,1,0:T(8,128)(2,1)S(1)}, u32[]{:S(2)}, u32[]{:S(2)}) collective-permute-start(bf16[4,144,256]{2,1,0:T(8,128)(2,1)S(1)} %get-tuple-element.102), channel_id=1, source_target_pairs={{0,4},{2,6},{4,0},{6,2},{8,12},{10,14},{12,8},{14,10},{16,20},{18,... | collective-permute-start | bytes 884744 | tf_op jit(solution)/shard_map/ppermute | solution.py:30
  56.0 8.8 %collective-permute-start.14 = (bf16[4,144,256]{2,1,0:T(8,128)(2,1)S(1)}, bf16[4,144,256]{2,1,0:T(8,128)(2,1)S(1)}, u32[]{:S(2)}, u32[]{:S(2)}) collective-permute-start(bf16[4,144,256]{2,1,0:T(8,128)(2,1)S(1)} %get-tuple-element.107), channel_id=1, source_target_pairs={{0,8},{2,10},{4,12},{6,14},{8,0},{10,2},{12,4},{14,6},{16,24},{18,... | collective-permute-start | bytes 884744 | tf_op jit(solution)/shard_map/ppermute | solution.py:30
  63.2 5.4 %collective-permute-start.20 = (bf16[2,160,256]{2,1,0:T(8,128)(2,1)S(1)}, bf16[2,160,256]{2,1,0:T(8,128)(2,1)S(1)}, u32[]{:S(2)}, u32[]{:S(2)}) collective-permute-start(bf16[2,160,256]{2,1,0:T(8,128)(2,1)S(1)} %get-tuple-element.118), channel_id=1, source_target_pairs={{0,4},{2,6},{4,0},{6,2},{8,12},{10,14},{12,8},{14,10},{16,20},{18,... | collective-permute-start | bytes 491528 | tf_op jit(solution)/shard_map/ppermute | solution.py:30
  64.2 7.7 %collective-permute-start.15 = (bf16[2,144,256]{2,1,0:T(8,128)(2,1)S(1)}, bf16[2,144,256]{2,1,0:T(8,128)(2,1)S(1)}, u32[]{:S(2)}, u32[]{:S(2)}) collective-permute-start(bf16[2,144,256]{2,1,0:T(8,128)(2,1)S(1)} %get-tuple-element.109), channel_id=1, source_target_pairs={{0,8},{2,10},{4,12},{6,14},{8,0},{10,2},{12,4},{14,6},{16,24},{18,... | collective-permute-start | bytes 442376 | tf_op jit(solution)/shard_map/ppermute | solution.py:30
  64.9 7.0 %collective-permute-start.16 = (bf16[2,144,256]{2,1,0:T(8,128)(2,1)S(1)}, bf16[2,144,256]{2,1,0:T(8,128)(2,1)S(1)}, u32[]{:S(2)}, u32[]{:S(2)}) collective-permute-start(bf16[2,144,256]{2,1,0:T(8,128)(2,1)S(1)} %get-tuple-element.110), channel_id=1, source_target_pairs={{0,2},{2,0},{4,6},{6,4},{8,10},{10,8},{12,14},{14,12},{16,18},{18,... | collective-permute-start | bytes 442376 | tf_op jit(solution)/shard_map/ppermute | solution.py:30
  68.7 10.5 %collective-permute-start.21 = (bf16[1,160,256]{2,1,0:T(8,128)(2,1)S(1)}, bf16[1,160,256]{2,1,0:T(8,128)(2,1)S(1)}, u32[]{:S(2)}, u32[]{:S(2)}) collective-permute-start(bf16[1,160,256]{2,1,0:T(8,128)(2,1)S(1)} %get-tuple-element.120), channel_id=1, source_target_pairs={{0,16},{2,18},{4,20},{6,22},{8,24},{10,26},{12,28},{14,30},{16,0},... | collective-permute-start | bytes 245768 | tf_op jit(solution)/shard_map/ppermute | solution.py:30
  72.0 10.2 %collective-permute-start.17 = (bf16[1,288,256]{2,1,0:T(8,128)(2,1)S(1)}, bf16[1,288,256]{2,1,0:T(8,128)(2,1)S(1)}, u32[]{:S(2)}, u32[]{:S(2)}) collective-permute-start(bf16[1,288,256]{2,1,0:T(8,128)(2,1)S(1)} %get-tuple-element.112), channel_id=1, source_target_pairs={{0,16},{2,18},{4,20},{6,22},{8,24},{10,26},{12,28},{14,30},{16,0},... | collective-permute-start | bytes 442376 | tf_op jit(solution)/shard_map/ppermute | solution.py:30
  79.3 1.4 %collective-permute-start.22 = (bf16[160,256]{1,0:T(8,128)(2,1)S(1)}, bf16[160,256]{1,0:T(8,128)(2,1)S(1)}, u32[]{:S(2)}, u32[]{:S(2)}) collective-permute-start(bf16[160,256]{1,0:T(8,128)(2,1)S(1)} %get-tuple-element.121.refs_0_), channel_id=1, source_target_pairs={{0,1},{1,0},{2,3},{3,2},{4,5},{5,4},{6,7},{7,6},{8,9},{9,8},{10,11... | collective-permute-start | bytes 245768 | tf_op jit(solution)/shard_map/ppermute | solution.py:30
  82.4 2.5 %collective-permute-start.23 = (bf16[288,256]{1,0:T(8,128)(2,1)S(1)}, bf16[288,256]{1,0:T(8,128)(2,1)S(1)}, u32[]{:S(2)}, u32[]{:S(2)}) collective-permute-start(bf16[288,256]{1,0:T(8,128)(2,1)S(1)} %get-tuple-element.136.refs_0_), channel_id=1, source_target_pairs={{0,1},{1,0},{2,3},{3,2},{4,5},{5,4},{6,7},{7,6},{8,9},{9,8},{10,11... | collective-permute-start | bytes 442376 | tf_op jit(solution)/shard_map/ppermute | solution.py:30
  (5 other events, 43.9 us)
